TPU v7x, 32 devices: a whole 2x2x4 slice. The times are simulated.
32 devices in a mesh: groups: 2 (over y), pair: 4 (over z), amp: 2 (over x), rep: 2 (over core).
Axes of the slice: x: 2, y: 2, z: 4, core: 2. Of those that a mesh axis runs over, the one named last changes fastest.
Arguments:
- amplitudes: float32 [4, 1728, 768], P('groups', 'pair', 'amp'), parts along dimension 0, may hold values from -8 to 8
- integrals: float32 [4, 1728, 2048], P('groups', 'pair', 'rep'), parts along dimension 0, may hold values from -0.21875 to 0.21875
- tile_map: int32 [4, 108], P('groups'), parts along dimension 0, may hold values from 0 to 107, as said below
- residual: float32 [2, 1024, 4, 768], P('rep', 'pair', 'groups', 'amp'), parts along dimension 2, may hold values from -8 to 8
Outputs:
- ladder: float32 [2, 1024, 4, 768], P('rep', 'pair', 'groups', 'amp'), parts along dimension 2
There are 2 independent parts, one for each index of `groups`. A program takes and returns all parts, laid end to end along the dimension named above; each array names one. Nothing has to cross between parts.
Inputs may be any that keep to these rules, and one draw needn't show every extreme that they name: For each irrep, tile_map names every block 0 to 107 exactly once. Split the entries into runs of 27 (the blocks stored on one index of pair) and the block numbers into ranges of 27: each run takes between 6 and 7 blocks from each range, and 7 from some range.
All inputs are finite; a program needn't handle non-finite values.
Results may differ from a plain program's by a relative error of at most 0.0001.
Values sent between devices are 32-bit elements; how exact they have to be, the bound alone decides.
A program may use at most 64 MiB of HBM per device.

v0:
```python
import jax
import jax.numpy as jnp
from jax import lax
from jax.sharding import PartitionSpec as P

TILE = 16


precise = lax.Precision.HIGHEST


def slot_plan(tile_ids, n_pair, slot_count, most_each):
    home_of = (tile_ids // slot_count).reshape(n_pair, slot_count)
    onehot = (home_of[:, :, None] == jnp.arange(n_pair, dtype=jnp.int32)[None, None, :]).astype(
        jnp.int32
    )
    before = jnp.cumsum(onehot, axis=1) - onehot
    rank_in = jnp.sum(before * onehot, axis=2)
    wanted = (
        rank_in[:, :, None, None] == jnp.arange(most_each, dtype=jnp.int32)[None, None, None, :]
    ).astype(jnp.int32)
    matched = onehot[:, :, :, None] * wanted
    source = jnp.sum(matched * jnp.arange(slot_count, dtype=jnp.int32)[None, :, None, None], axis=1)
    filled = jnp.sum(matched, axis=1)
    return (home_of, rank_in, source, filled)


def local(amplitudes, integrals, tile_map, residual):
    n_pair = lax.axis_size("pair")
    device = lax.axis_index("pair")
    slot_count = integrals.shape[1] // TILE
    most_each = (slot_count + n_pair - 1) // n_pair
    occ_count = amplitudes.shape[2]
    plans = [slot_plan(tile_map[irrep], n_pair, slot_count, most_each) for irrep in range(2)]
    outgoing = []
    for irrep in range(2):
        home_of, rank_in, source, filled = plans[irrep]
        dest_slots = jnp.take(source, device, axis=1)
        dest_fill = jnp.take(filled, device, axis=1)
        stored_ids = jnp.take_along_axis(
            tile_map[irrep].reshape(n_pair, slot_count), dest_slots, axis=1
        )
        local_tile = jnp.where(dest_fill > 0, stored_ids - device * slot_count, 0)
        amp_blocks = amplitudes[irrep].reshape(slot_count, TILE, occ_count)
        chosen = amp_blocks[local_tile] * dest_fill[:, :, None, None].astype(jnp.float32)
        outgoing.append(chosen.reshape(n_pair, most_each * TILE, occ_count))
    arrived = lax.all_to_all(jnp.stack(outgoing), "pair", split_axis=1, concat_axis=1, tiled=True)
    picked_rows = []
    for irrep in range(2):
        home_of, rank_in, source, filled = plans[irrep]
        block_index = jnp.take(home_of, device, axis=0) * most_each + jnp.take(
            rank_in, device, axis=0
        )
        received = arrived[irrep].reshape(n_pair * most_each, TILE, occ_count)
        picked_rows.append(received[block_index].reshape(slot_count * TILE, occ_count))
    amp_rows = jnp.stack(picked_rows)
    summed = lax.psum_scatter(
        jnp.einsum(
            "gkw,gko->wgo",
            integrals,
            amp_rows,
            precision=precise,
            preferred_element_type=jnp.float32,
        ),
        "pair",
        scatter_dimension=0,
        tiled=True,
    )
    return residual + 0.5 * summed[None]


def solution(mesh):
    placed = (
        P("groups", "pair", "amp"),
        P("groups", "pair", "rep"),
        P("groups", None),
        P("rep", "pair", "groups", "amp"),
    )
    return jax.shard_map(
        local,
        mesh=mesh,
        in_specs=placed,
        out_specs=P("rep", "pair", "groups", "amp"),
        check_vma=False,
    )
```

profile of v0, /device:TPU:0, one launch (start us, length us, event | category | flops | bytes accessed | tf_op | source)
XLA Modules:
  0.0 175.2 jit_solution(3442484592112860182)
XLA Ops:
  6.5 0.9 slice_reduce_fusion.1
  7.4 0.1 squeeze.6
  7.5 0.1 squeeze.7
  7.6 0.6 add_select_fusion
  8.2 0.6 copy-done.4
  8.8 0.7 fusion.4
  9.5 0.9 copy.15
  10.4 1.5 reduce_window_sum.17
  11.9 1.4 fusion.3
  13.3 1.5 reduce_window_sum.18
  14.8 1.5 copy.16
  16.3 1.1 select_reduce_fusion.1
  17.4 0.0 copy-start.6
  17.4 0.6 copy-done.6
  18.0 0.6 fusion.7
  18.6 2.3 %multiply_reduce_fusion.1 = (s32[4,4,7]{1,2,0:T(8,128)}, s32[4,4,7]{1,2,0:T(8,128)S(1)}) fusion(s32[4,27,7]{1,2,0:T(8,128)} %fusion.7, s32[4,27,4]{1,2,0:T(4,128)S(1)} %copy.15), kind=kLoop, calls=%fused_computation.17 | loop fusion | flops 11872 | bytes 5648 | tf_op jit(solution)/shard_map/reduce_sum | solution.py:24
  20.9 0.2 select_reduce_fusion.4
  21.2 0.0 copy-start.5
  21.2 0.6 copy-done.5
  21.8 0.1 reshape.331
  21.8 1.3 gather_fusion.4
  23.2 0.7 reshape.334
  23.9 0.9 select_reduce_fusion.5
  24.8 1.3 fusion.24
  26.1 0.8 reshape.280
  26.9 0.6 pad_clamp_fusion.3
  27.5 2.4 %fusion.23 = (f32[1,432,384]{2,1,0:T(8,128)}, f32[1,432,384]{2,1,0:T(8,128)}) fusion(f32[2,432,384]{2,1,0:T(8,128)} %param.10), kind=kLoop, calls=%fused_computation.79 | loop fusion | bytes 2654208 | tf_op jit(solution)/shard_map/slice | solution.py:44
  29.9 0.0 copy-done.11
  29.9 0.7 mul.112
  30.6 1.4 mul.113
  31.9 1.1 select_reduce_fusion
  33.0 0.0 copy-start.7
  33.0 0.6 copy-done.7
  33.6 0.0 copy-done.2
  33.6 1.2 multiply_reduce_fusion
  34.8 0.2 select_reduce_fusion.2
  35.0 0.1 reshape.338
  35.1 0.9 gather_fusion.5
  35.9 0.1 reshape.341
  36.0 0.9 select_reduce_fusion.3
  37.0 0.6 fusion.25
  37.5 0.1 reshape.288
  37.6 0.6 pad_clamp_fusion.2
  38.2 0.8 mul.122
  39.0 0.7 mul.123
  39.6 2.7 %gather_fusion = f32[28,16,384]{2,1,0:T(8,128)} fusion(f32[27,16,384]{2,1,0:T(8,128)} %bitcast.50, s32[1024]{0:T(1024)} %pad_clamp_fusion.3), kind=kCustom, calls=%fused_computation.2 | custom fusion | bytes 1376368 | tf_op jit(solution)/shard_map/gather | solution.py:45
  42.3 2.1 %broadcast_multiply_fusion.1 = f32[1,4,112,384]{3,2,0,1:T(8,128)} fusion(f32[1,4,112,384]{3,2,0,1:T(8,128)} %bitcast.51, f32[4,112]{1,0:T(4,128)S(1)} %copy-done.9), kind=kLoop, calls=%fused_computation.13 | loop fusion | flops 172032 | bytes 1378048 | tf_op jit(solution)/shard_map/mul | solution.py:45
  44.4 2.5 %gather_fusion.1 = f32[28,16,384]{2,1,0:T(8,128)} fusion(f32[27,16,384]{2,1,0:T(8,128)} %bitcast.49, s32[1024]{0:T(1024)S(1)} %copy-done.8), kind=kCustom, calls=%fused_computation.3 | custom fusion | bytes 1376368 | tf_op jit(solution)/shard_map/gather | solution.py:45
  46.9 1.3 broadcast_multiply_fusion
  48.2 0.0 copy-done.1
  48.2 1.2 pad_maximum_fusion
  49.4 6.3 %all-to-all-start = ((f32[2,4,112,384]{3,2,0,1:T(8,128)}), f32[2,4,112,384]{3,2,0,1:T(8,128)}, u32[]{:S(2)}, u32[]{:S(2)}) async-start(f32[2,4,112,384]{3,2,0,1:T(8,128)} %pad_maximum_fusion), calls=%async_computation | async-start | bytes 2752512 | tf_op jit(solution)/shard_map/all_to_all | solution.py:47
  55.7 0.7 compare_select_fusion.5
  56.4 0.7 compare_select_fusion.4
  57.1 31.4 %all-to-all-done = f32[2,4,112,384]{3,2,0,1:T(8,128)} async-done(((f32[2,4,112,384]{3,2,0,1:T(8,128)}), f32[2,4,112,384]{3,2,0,1:T(8,128)}, u32[]{:S(2)}, u32[]{:S(2)}) %all-to-all-start) | async-done | bytes 1376288 | tf_op jit(solution)/shard_map/all_to_all | solution.py:47
  88.6 2.5 %fusion.22 = (f32[1,4,112,384]{3,2,0,1:T(8,128)}, f32[1,4,112,384]{3,2,0,1:T(8,128)}) fusion(f32[2,4,112,384]{3,2,0,1:T(8,128)} %all-to-all-done), kind=kLoop, calls=%fused_computation.78 | loop fusion | bytes 2752512 | tf_op jit(solution)/shard_map/slice | solution.py:54
  91.1 2.5 %gather_fusion.2 = f32[27,16,384]{2,1,0:T(8,128)} fusion(f32[28,16,384]{2,1,0:T(8,128)} %bitcast.54, s32[1024]{0:T(1024)S(1)} %pad_clamp_fusion.1), kind=kCustom, calls=%fused_computation.4 | custom fusion | bytes 1327212 | tf_op jit(solution)/shard_map/gather | solution.py:55
  93.6 2.5 %gather_fusion.3 = f32[27,16,384]{2,1,0:T(8,128)} fusion(f32[28,16,384]{2,1,0:T(8,128)} %bitcast.53, s32[1024]{0:T(1024)S(1)} %pad_clamp_fusion), kind=kCustom, calls=%fused_computation.5 | custom fusion | bytes 1327212 | tf_op jit(solution)/shard_map/gather | solution.py:55
  96.2 8.2 %convolution_bitcast_fusion = f32[1024,2,384]{0,2,1:T(8,128)} fusion(f32[2,432,1024]{2,1,0:T(8,128)S(1)} %copy-done, f32[1,432,384]{2,1,0:T(8,128)} %bitcast.56, f32[1,432,384]{2,1,0:T(8,128)} %bitcast.55), kind=kOutput, calls=%fused_computation.6 | convolution fusion | flops 4077195264 | bytes 8011776 | tf_op jit(solution)/shard_map/gkw,gko->wgo/dot_general | solution.py:58
  104.3 0.0 reduce-scatter.2.cloned.1.call-update
  104.4 2.1 %copy.17 = f32[1,256,2,384]{1,3,2,0:T(8,128)} copy(f32[1,256,2,384]{3,2,1,0:T(2,128)} %param.13) | data formatting | bytes 1572864 | tf_op args[3]
  106.5 57.4 %reduce-scatter.2.cloned.1.call-done = f32[256,2,384]{0,2,1:T(8,128)} async-done(((f32[1024,2,384]{0,2,1:T(8,128)}), f32[256,2,384]{0,2,1:T(8,128)}) %reduce-scatter.2.cloned.1.call-update) | async-done | bytes 786448 | tf_op jit(solution)/shard_map/reduce_scatter | solution.py:57
  163.9 2.3 %bitcast_add_fusion = f32[1,256,2,384]{1,3,2,0:T(8,128)} fusion(f32[1,256,2,384]{1,3,2,0:T(8,128)} %copy.17, f32[256,2,384]{0,2,1:T(8,128)} %reduce-scatter.2.cloned.1.call-done), kind=kLoop, calls=%fused_computation.11 | loop fusion | flops 393216 | bytes 2359296 | tf_op jit(solution)/shard_map/add | solution.py:69
  166.2 2.1 %copy.18 = f32[1,256,2,384]{3,2,1,0:T(2,128)} copy(f32[1,256,2,384]{1,3,2,0:T(8,128)} %bitcast_add_fusion) | data formatting | bytes 1572864 | tf_op jit(solution)/shard_map/add | solution.py:69
  (20 shorter events, 0.1 us)
Async XLA Ops:
  6.5 89.6 %copy-start = (f32[2,432,1024]{2,1,0:T(8,128)S(1)}, f32[2,432,1024]{2,1,0:T(8,128)}, u32[]{:S(2)}) copy-start(f32[2,432,1024]{2,1,0:T(8,128)} %param.11) | copy-start | bytes 10616836
  8.2 0.6 copy-start.4
  17.4 0.6 copy-start.6
  21.2 0.6 copy-start.5
  23.2 8.8 %copy-start.3 = (s32[4,27]{1,0:T(4,128)S(1)}, s32[4,27]{1,0:T(4,128)}, u32[]{:S(2)}) copy-start(s32[4,27]{1,0:T(4,128)} %get-tuple-element.44) | copy-start | bytes 1300
  26.9 3.0 %copy-start.11 = (f32[4,7]{1,0:T(4,128)S(1)}, f32[4,7]{1,0:T(4,128)}, u32[]{:S(2)}) copy-start(f32[4,7]{1,0:T(4,128)} %get-tuple-element.40) | copy-start | bytes 340
  27.4 6.2 %copy-start.2 = (s32[4,27,4]{1,2,0:T(4,128)S(1)}, s32[4,27,4]{1,2,0:T(4,128)}, u32[]{:S(2)}) copy-start(s32[4,27,4]{1,2,0:T(4,128)} %copy.16) | copy-start | bytes 5188
  33.0 0.6 copy-start.7
  39.6 2.7 %copy-start.9 = (f32[4,112]{1,0:T(4,128)S(1)}, f32[4,112]{1,0:T(4,128)}, u32[]{:S(2)}) copy-start(f32[4,112]{1,0:T(4,128)} %mul.113) | copy-start | bytes 5380
  39.6 4.7 %copy-start.8 = (s32[1024]{0:T(1024)S(1)}, s32[1024]{0:T(1024)}, u32[]{:S(2)}) copy-start(s32[1024]{0:T(1024)} %pad_clamp_fusion.2) | copy-start | bytes 12292
  42.3 4.6 %copy-start.10 = (f32[4,112]{1,0:T(4,128)S(1)}, f32[4,112]{1,0:T(4,128)}, u32[]{:S(2)}) copy-start(f32[4,112]{1,0:T(4,128)} %mul.123) | copy-start | bytes 5380
  46.9 1.3 copy-start.1
  49.4 39.2 %all-to-all-start = ((f32[2,4,112,384]{3,2,0,1:T(8,128)}), f32[2,4,112,384]{3,2,0,1:T(8,128)}, u32[]{:S(2)}, u32[]{:S(2)}) async-start(f32[2,4,112,384]{3,2,0,1:T(8,128)} %pad_maximum_fusion), calls=%async_computation | async-start | bytes 2752512 | tf_op jit(solution)/shard_map/all_to_all | solution.py:47
  55.7 108.1 %reduce-scatter.2.cloned.1.call-start = ((), (), s32[]{:S(2)}) async-start(), calls=%async_computation.2 | async-start | bytes 3932160 | tf_op jit(solution)/shard_map/reduce_scatter | solution.py:57
Sparse Core Ops, SparseCore 0:
  104.5 59.3 reduce-scatter.1
where the time goes:
time: 176 us; the launch traced here: 175 us
  waiting for transfers between devices  88.9 us (51%)
  local copies, waits for them, and re-layouts  32.7 us (19%)
  other arithmetic  25.6 us (15%)
  between operations  13.5 us (8%)
  matrix products  8.17 us (5%)
  starting transfers between devices  6.32 us (4%)
    reduce_scatter x1, waiting for transfers between devices, local(): lax.psum_scatter(jnp.einsum('gkw,gko->wgo', integrals, amp_rows, precisio...  57.4 us
    all_to_all x1, waiting for transfers between devices, local(): lax.all_to_all(jnp.stack(outgoing), 'pair', split_axis=1, concat_axis=1,...  31.4 us
    dot_general x1, matrix products, local(): jnp.einsum('gkw,gko->wgo', integrals, amp_rows, precision=precise, prefer...  8.17 us
    all_to_all x1, starting transfers between devices, local(): lax.all_to_all(jnp.stack(outgoing), 'pair', split_axis=1, concat_axis=1,...  6.32 us
    gather x2, local copies, waits for them, and re-layouts, local(): amp_blocks[local_tile] * dest_fill[:, :, None, None].astype(jnp.float32)  5.18 us
    gather x2, local copies, waits for them, and re-layouts, local(): received[block_index].reshape(slot_count * TILE, occ_count)  5.06 us
    unnamed x25, local copies, waits for them, and re-layouts  4.48 us
  transfers between devices with their start and end apart: 2, of which 2 were waited for; matrix products, arithmetic and copies ran while one was open for 2% of the time, Pallas kernels for 0%

commit v1 on v0

v1 whole, which is shorter than its diff:
```python
import functools

import jax
import jax.numpy as jnp
from jax import lax
from jax.experimental import pallas as pl
from jax.experimental.pallas import tpu as pltpu
from jax.sharding import PartitionSpec as P

TILE = 16
HALF = TILE // 2
BLOCKS = 4
MESH = pl.DeviceIdType.MESH


def table_kernel(n, most, map_ref, send_ref, pick_ref, count_ref):
    me = lax.axis_index("pair")
    slots = map_ref.shape[1] // n
    scale = ((1 << 20) + slots - 1) // slots
    low = me * slots

    for g in range(2):

        @pl.loop(0, n)
        def _(d):
            for j in range(most + 1):
                send_ref[g, d * (most + 1) + j] = 0
            found = jnp.int32(0)
            for k in range(slots):
                tile = map_ref[g, d * slots + k]
                mine = (tile >= low) & (tile < low + slots)
                send_ref[g, d * (most + 1) + found] = jnp.where(mine, tile - low, 0)
                found = found + mine.astype(jnp.int32)
            count_ref[d] = 0

        for k in range(slots):
            tile = map_ref[g, low + k]
            home = lax.shift_right_logical(tile * scale, 20)
            rank = count_ref[home]
            pick_ref[g, k] = home * most + rank
            count_ref[home] = rank + 1


def split(x):
    high = x.astype(jnp.bfloat16)
    return high, (x - high.astype(jnp.float32)).astype(jnp.bfloat16)


def ladder_kernel(
    n,
    most,
    send_tab,
    pick_tab,
    amps,
    ints_hbm,
    out,
    ints,
    packed,
    pool0,
    pool1,
    ints_hi,
    ints_lo,
    amp_hi,
    amp_lo,
    part,
    from_left,
    from_right,
    load_sem,
    a_send,
    a_recv,
    s_send,
    s_recv,
    r_send,
    r_recv,
    l_send,
    l_recv,
):
    me = lax.axis_index("pair")
    core = lax.axis_index("rep")
    slots = amps.shape[1]
    rows = part.shape[1]
    block = rows // BLOCKS
    chunk = rows // n
    per_block = n // BLOCKS
    pools = (pool0, pool1)

    loads = [pltpu.make_async_copy(ints_hbm.at[g], ints.at[g], load_sem.at[g]) for g in range(2)]
    for load in loads:
        load.start()

    barrier = pltpu.get_barrier_semaphore()

    @pl.loop(1, n)
    def _(off):
        pl.semaphore_signal(
            barrier, inc=1, device_id={"pair": lax.rem(me + off, n)}, device_id_type=MESH
        )

    pl.semaphore_signal(barrier, inc=1, device_id={"rep": 1 - core}, device_id_type=MESH)

    def pack(g):
        @pl.loop(1, n)
        def _(off):
            d = lax.rem(me + off, n)
            for j in range(most):
                packed[g, off, j] = amps[g, send_tab[g, d * (most + 1) + j], core]

    def exchange(g, off):
        source = lax.rem(me - off + n, n)
        target = lax.rem(me + off, n)
        return (
            pltpu.make_async_remote_copy(
                src_ref=packed.at[g, off],
                dst_ref=pools[g].at[core, pl.ds(me * most, most)],
                send_sem=a_send.at[g, off],
                recv_sem=a_recv.at[g, off],
                device_id={"pair": target},
                device_id_type=MESH,
            ),
            pltpu.make_async_remote_copy(
                src_ref=pools[g].at[core, pl.ds(source * most, most)],
                dst_ref=pools[g].at[core, pl.ds(source * most, most)],
                send_sem=s_send.at[g, off],
                recv_sem=s_recv.at[g, off],
                device_id={"rep": 1 - core},
                device_id_type=MESH,
            ),
        )

    pack(0)
    pl.semaphore_wait(barrier, n)
    for g in range(2):
        if g == 1:
            pack(1)

        @pl.loop(1, n)
        def _(off):
            exchange(g, off)[0].start()

    for g in range(2):
        for j in range(most):
            for h in range(2):
                pools[g][h, me * most + j] = amps[g, send_tab[g, me * (most + 1) + j], h]

    for g in range(2):
        loads[g].wait()

        @pl.loop(0, BLOCKS)
        def _(b):
            columns = pl.ds(pl.multiple_of(b * block, block), block)
            high, low = split(ints[g, :, columns].T)
            ints_hi[g, columns, :] = high
            ints_lo[g, columns, :] = low

    def send_right(g, t, src):
        return pltpu.make_async_remote_copy(
            src_ref=src,
            dst_ref=from_left.at[g, t],
            send_sem=r_send.at[g, t],
            recv_sem=r_recv.at[g, t],
            device_id={"pair": lax.rem(me + 1, n)},
            device_id_type=MESH,
        )

    def send_left(g, t, src):
        return pltpu.make_async_remote_copy(
            src_ref=src,
            dst_ref=from_right.at[g, t],
            send_sem=l_send.at[g, t],
            recv_sem=l_recv.at[g, t],
            device_id={"pair": lax.rem(me - 1 + n, n)},
            device_id_type=MESH,
        )

    def own(t):
        return pl.ds(pl.multiple_of(t * chunk, chunk), chunk)

    for g in range(2):

        @pl.loop(1, n)
        def _(off):
            arrive, pass_on = exchange(g, off)
            arrive.wait_recv()
            pass_on.start()

        @pl.loop(1, n)
        def _(off):
            exchange(g, off)[1].wait_recv()

        @pl.loop(0, slots)
        def _(k):
            where = pick_tab[g, k]
            tile = jnp.concatenate([pools[g][0, where], pools[g][1, where]], axis=0)
            high, low = split(tile)
            at = pl.ds(pl.multiple_of(k * TILE, TILE), TILE)
            amp_hi[g, at, :] = high
            amp_lo[g, at, :] = low

        @pl.loop(0, BLOCKS)
        def _(i):
            b = jnp.where(me < n // 2, BLOCKS - 1 - i, i)
            at = pl.ds(pl.multiple_of(b * block, block), block)
            dot = functools.partial(jnp.dot, preferred_element_type=jnp.float32)
            part[g, at, :] = (
                dot(ints_hi[g, at, :], amp_lo[g])
                + dot(ints_lo[g, at, :], amp_hi[g])
                + dot(ints_hi[g, at, :], amp_hi[g])
            )

            @pl.loop(0, per_block)
            def _(j):
                t = b * per_block + jnp.where(me < n // 2, per_block - 1 - j, j)

                @pl.when((me == 0) & (t > 0))
                def _():
                    send_right(g, t, part.at[g, own(t)]).start()

                @pl.when((me == n - 1) & (t < n - 1))
                def _():
                    send_left(g, t, part.at[g, own(t)]).start()

    def forward_right(g, t):
        @pl.when((t > me) & (me > 0))
        def _():
            copy = send_right(g, t, from_left.at[g, t])
            copy.wait_recv()
            from_left[g, t] = from_left[g, t] + part[g, own(t), :]
            copy.start()

    def forward_left(g, t):
        @pl.when((t < me) & (me < n - 1))
        def _():
            copy = send_left(g, t, from_right.at[g, t])
            copy.wait_recv()
            from_right[g, t] = from_right[g, t] + part[g, own(t), :]
            copy.start()

    for g in range(2):

        @pl.loop(0, n)
        def _(i):
            @pl.when(me < n // 2)
            def _():
                forward_right(g, n - 1 - i)
                forward_left(g, i)

            @pl.when(me >= n // 2)
            def _():
                forward_left(g, i)
                forward_right(g, n - 1 - i)

    for g in range(2):
        out[g] = part[g, own(me), :]

        @pl.when(me > 0)
        def _():
            send_right(g, me, from_left.at[g, me]).wait_recv()
            out[g] = out[g] + from_left[g, me]

        @pl.when(me < n - 1)
        def _():
            send_left(g, me, from_right.at[g, me]).wait_recv()
            out[g] = out[g] + from_right[g, me]

    for g in range(2):

        @pl.loop(1, n)
        def _(off):
            arrive, pass_on = exchange(g, off)
            arrive.wait_send()
            pass_on.wait_send()

        @pl.loop(0, n)
        def _(t):
            @pl.when(t > me)
            def _():
                send_right(g, t, from_left.at[g, t]).wait_send()

            @pl.when(t < me)
            def _():
                send_left(g, t, from_right.at[g, t]).wait_send()


def local(n, amplitudes, integrals, tile_map, residual):
    depth, occ = amplitudes.shape[1:]
    rows = integrals.shape[2]
    slots = depth // TILE
    most = (slots + n - 1) // n
    chunk = rows // n
    smem = pl.BlockSpec(memory_space=pltpu.SMEM)
    vmem = pl.BlockSpec(memory_space=pltpu.VMEM)
    send_tab, pick_tab = pl.pallas_call(
        functools.partial(table_kernel, n, most),
        out_shape=(
            jax.ShapeDtypeStruct((2, n * (most + 1)), jnp.int32),
            jax.ShapeDtypeStruct((2, slots), jnp.int32),
        ),
        in_specs=[smem],
        out_specs=(smem, smem),
        scratch_shapes=[pltpu.SMEM((n,), jnp.int32)],
    )(tile_map)
    f32, bf16 = jnp.float32, jnp.bfloat16
    dma = pltpu.SemaphoreType.DMA
    flops = 2 * 3 * 2 * depth * rows * occ
    summed = pl.pallas_call(
        functools.partial(ladder_kernel, n, most),
        out_shape=jax.ShapeDtypeStruct((2, chunk, occ), f32),
        in_specs=[smem, smem, vmem, pl.BlockSpec(memory_space=pl.ANY)],
        out_specs=vmem,
        scratch_shapes=[
            pltpu.VMEM((2, depth, rows), f32),
            pltpu.VMEM((2, n, most, HALF, occ), f32),
            pltpu.VMEM((2, n * most, HALF, occ), f32),
            pltpu.VMEM((2, n * most, HALF, occ), f32),
            pltpu.VMEM((2, rows, depth), bf16),
            pltpu.VMEM((2, rows, depth), bf16),
            pltpu.VMEM((2, depth, occ), bf16),
            pltpu.VMEM((2, depth, occ), bf16),
            pltpu.VMEM((2, rows, occ), f32),
            pltpu.VMEM((2, n, chunk, occ), f32),
            pltpu.VMEM((2, n, chunk, occ), f32),
            dma((2,)),
        ]
        + [dma((2, n))] * 8,
        compiler_params=pltpu.CompilerParams(
            collective_id=0, has_side_effects=True, vmem_limit_bytes=56 * 1024 * 1024
        ),
        cost_estimate=pl.CostEstimate(
            flops=flops, bytes_accessed=4 * (integrals.size + amplitudes.size), transcendentals=0
        ),
    )(
        send_tab,
        pick_tab,
        amplitudes.reshape(2, slots, 2, HALF, occ),
        integrals,
    )
    return residual + 0.5 * jnp.transpose(summed, (1, 0, 2))[None]


def solution(mesh):
    placed = (
        P("groups", "pair", "amp"),
        P("groups", "pair", "rep"),
        P("groups", None),
        P("rep", "pair", "groups", "amp"),
    )
    return jax.shard_map(
        functools.partial(local, mesh.shape["pair"]),
        mesh=mesh,
        in_specs=placed,
        out_specs=P("rep", "pair", "groups", "amp"),
        check_vma=False,
    )
```

time: 176 us -> 84.6 us (0.48)
  waiting for transfers between devices: 88.9 us -> 0 us
  Pallas kernels: 0 us -> 81.7 us
  local copies, waits for them, and re-layouts: 32.7 us -> 1.49 us
  other arithmetic: 25.6 us -> 1.23 us
  between operations: 13.5 us -> 0.04 us
  matrix products: 8.17 us -> 0 us
  starting transfers between devices: 6.32 us -> 0 us
    pallas_call x0 -> x2, Pallas kernels: none -> 81.7 us  [the longest x1 79 us: local(): pl.pallas_call(functools.partial(ladder_kernel, n, most), out_shape=jax.S...]
    reduce_scatter x1 -> x0, waiting for transfers between devices: 57.4 us -> none  [local(): lax.psum_scatter(jnp.einsum('gkw,gko->wgo', integrals, amp_rows, precisio...]
    all_to_all x1 -> x0, waiting for transfers between devices: 31.4 us -> none  [local(): lax.all_to_all(jnp.stack(outgoing), 'pair', split_axis=1, concat_axis=1,...]
    gather x10 -> x0, local copies, waits for them, and re-layouts: 13.4 us -> none  [the longest x2 5.18 us: local(): amp_blocks[local_tile] * dest_fill[:, :, None, None].astype(jnp.float32)]
    dot_general x1 -> x0, matrix products: 8.17 us -> none  [local(): jnp.einsum('gkw,gko->wgo', integrals, amp_rows, precision=precise, prefer...]
    all_to_all x1 -> x0, starting transfers between devices: 6.32 us -> none  [local(): lax.all_to_all(jnp.stack(outgoing), 'pair', split_axis=1, concat_axis=1,...]
    slice x3 -> x0, local copies, waits for them, and re-layouts: 5.83 us -> none  [the longest x1 2.52 us: local(): received = arrived[irrep].reshape(n_pair * most_each, TILE, occ_count)]
    reduce_sum x4 -> x0, other arithmetic: 5.6 us -> none  [the longest x2 3.49 us: slot_plan(): filled = jnp.sum(matched, axis=1)]
  transfers between devices with their start and end apart: 2 -> 0, of which waited for: 2 -> 0; matrix products, arithmetic and copies ran while one was open for 2% -> 0% of each run, Pallas kernels for 0% -> 0%
where the time goes in v1:
time: 84.6 us; the launch traced here: 84.4 us
  Pallas kernels  81.7 us (97%)
  local copies, waits for them, and re-layouts  1.49 us (2%)
  other arithmetic  1.23 us (1%)
    pallas_call x1, Pallas kernels, local(): pl.pallas_call(functools.partial(ladder_kernel, n, most), out_shape=jax.S...  79 us
    pallas_call x1, Pallas kernels, local(): pl.pallas_call(functools.partial(table_kernel, n, most), out_shape=(jax.S...  2.68 us

profile of v1, /device:TPU:0, one launch (start us, length us, event | category | flops | bytes accessed | tf_op | source)
XLA Modules:
  0.0 84.4 jit_solution(13215962707531763532)
XLA Ops:
  0.0 2.7 %shard_map.46 = (s32[2,32]{1,0:T(2,128)}, s32[2,27]{1,0:T(2,128)}) custom-call(s32[2,108]{1,0:T(2,128)} %map_ref.1), custom_call_target="tpu_custom_call" | custom-call | tf_op jit(solution)/shard_map/pallas_call | solution.py:292
  2.7 0.0 copy-start
  2.7 79.0 %shard_map.47 = f32[2,256,384]{2,1,0:T(8,128)} custom-call(s32[2,32]{1,0:T(2,128)} %get-tuple-element.7.send_tab, s32[2,27]{1,0:T(2,128)} %get-tuple-element.8.pick_tab, f32[2,27,2,8,384]{4,3,2,1,0:T(8,128)} %bitcast.5, f32[2,432,1024]{2,1,0:T(8,128)} %ints_hbm.1), custom_call_target="tpu_custom_call" | custom-call | flops 2038431744 | bytes 4866048 | tf_op jit(solution)/shard_map/pallas_call | solution.py:305
  81.7 0.0 copy-done
  81.7 1.2 %bitcast_add_fusion = f32[1,256,2,384]{3,1,2,0:T(8,128)S(1)} fusion(f32[1,256,2,384]{3,2,1,0:T(2,128)S(1)} %copy-done, f32[2,256,384]{2,1,0:T(8,128)} %shard_map.47), kind=kLoop, calls=%fused_computation | loop fusion | flops 393216 | bytes 2359296 | tf_op jit(solution)/shard_map/add | solution.py:337
  82.9 1.5 %copy.6 = f32[1,256,2,384]{3,2,1,0:T(2,128)} copy(f32[1,256,2,384]{3,1,2,0:T(8,128)S(1)} %bitcast_add_fusion) | data formatting | bytes 1572864 | tf_op jit(solution)/shard_map/add | solution.py:337
Async XLA Ops:
  2.7 79.0 %copy-start = (f32[1,256,2,384]{3,2,1,0:T(2,128)S(1)}, f32[1,256,2,384]{3,2,1,0:T(2,128)}, u32[]{:S(2)}) copy-start(f32[1,256,2,384]{3,2,1,0:T(2,128)} %param.7) | copy-start | bytes 2359300

commit v2 on v1

--- a/solution.py
+++ b/solution.py
@@ -31,14 +31,20 @@
                 mine = (tile >= low) & (tile < low + slots)
                 send_ref[g, d * (most + 1) + found] = jnp.where(mine, tile - low, 0)
                 found = found + mine.astype(jnp.int32)
-            count_ref[d] = 0
-
-        for k in range(slots):
-            tile = map_ref[g, low + k]
-            home = lax.shift_right_logical(tile * scale, 20)
-            rank = count_ref[home]
-            pick_ref[g, k] = home * most + rank
-            count_ref[home] = rank + 1
+
+        runs = [(g, me)] if g == 0 else [(1, me), (2, jnp.where(me < n // 2, 0, n - 1))]
+        for row, run in runs:
+
+            @pl.loop(0, n)
+            def _(d):
+                count_ref[d] = 0
+
+            for k in range(slots):
+                tile = map_ref[g, run * slots + k]
+                home = lax.shift_right_logical(tile * scale, 20)
+                rank = count_ref[home]
+                pick_ref[row, k] = home * most + rank
+                count_ref[home] = rank + 1
 
 
 def split(x):
@@ -49,6 +55,7 @@
 def ladder_kernel(
     n,
     most,
+    proxy,
     send_tab,
     pick_tab,
     amps,
@@ -65,6 +72,12 @@
     part,
     from_left,
     from_right,
+    pool_end,
+    end_ints,
+    end_hi,
+    end_lo,
+    end_amp_hi,
+    end_amp_lo,
     load_sem,
     a_send,
     a_recv,
@@ -74,9 +87,25 @@
     r_recv,
     l_send,
     l_recv,
+    p_send,
+    p_recv,
+    q_send,
+    q_recv,
+    i_send,
+    i_recv,
+    x_send,
+    x_recv,
+    f_sem,
 ):
     me = lax.axis_index("pair")
     core = lax.axis_index("rep")
+    column = lax.axis_index("amp")
+    end = jnp.where(me < n // 2, 0, n - 1)
+    at_end = me == end
+    helper = jnp.clip(end, 1, n - 2)
+    is_helper = me == helper
+    first_right = (0, 1 if proxy else 0)
+    first_left = (n - 1, n - 2 if proxy else n - 1)
     slots = amps.shape[1]
     rows = part.shape[1]
     block = rows // BLOCKS
@@ -97,9 +126,11 @@
         )
 
     pl.semaphore_signal(barrier, inc=1, device_id={"rep": 1 - core}, device_id_type=MESH)
+    if proxy:
+        pl.semaphore_signal(barrier, inc=1, device_id={"amp": 1 - column}, device_id_type=MESH)
 
     def pack(g):
-        @pl.loop(1, n)
+        @pl.loop(0 if proxy and g == 1 else 1, n)
         def _(off):
             d = lax.rem(me + off, n)
             for j in range(most):
@@ -127,15 +158,110 @@
             ),
         )
 
+    def to_helper(off, d):
+        return pltpu.make_async_remote_copy(
+            src_ref=packed.at[1, off],
+            dst_ref=pool_end.at[core, pl.ds(me * most, most)],
+            send_sem=a_send.at[1, off],
+            recv_sem=p_recv.at[me],
+            device_id={"pair": jnp.clip(d, 1, n - 2)},
+            device_id_type=MESH,
+        )
+
+    def end_pass(home):
+        rows_at = (core, pl.ds(home * most, most))
+        return pltpu.make_async_remote_copy(
+            src_ref=pool_end.at[rows_at],
+            dst_ref=pool_end.at[rows_at],
+            send_sem=q_send.at[home],
+            recv_sem=q_recv.at[home],
+            device_id={"rep": 1 - core},
+            device_id_type=MESH,
+        )
+
+    others = (core, pl.ds(jnp.where(end == 0, most, 0), (n - 1) * most))
+
+    def to_end():
+        return pltpu.make_async_remote_copy(
+            src_ref=pool_end.at[others],
+            dst_ref=pool1.at[others],
+            send_sem=f_sem.at[0],
+            recv_sem=f_sem.at[1],
+            device_id={"pair": end},
+            device_id_type=MESH,
+        )
+
+    def end_share():
+        return pltpu.make_async_remote_copy(
+            src_ref=pool1.at[others],
+            dst_ref=pool1.at[others],
+            send_sem=f_sem.at[2],
+            recv_sem=f_sem.at[3],
+            device_id={"rep": 1 - core},
+            device_id_type=MESH,
+        )
+
+    half_rows = pl.ds(
+        pl.multiple_of(column * (slots * HALF), HALF), slots * HALF
+    )
+
+    def ints_piece(i):
+        b = jnp.where(end == 0, n - 1 - i, i)
+        return pltpu.make_async_remote_copy(
+            src_ref=ints_hbm.at[
+                1, half_rows, pl.ds(pl.multiple_of(b * chunk, chunk), chunk)
+            ],
+            dst_ref=end_ints.at[i, half_rows],
+            send_sem=i_send.at[i],
+            recv_sem=i_recv.at[i],
+            device_id={"pair": helper},
+            device_id_type=MESH,
+        )
+
+    def ints_across(i):
+        return pltpu.make_async_remote_copy(
+            src_ref=end_ints.at[i, half_rows],
+            dst_ref=end_ints.at[i, half_rows],
+            send_sem=x_send.at[i],
+            recv_sem=x_recv.at[i],
+            device_id={"amp": 1 - column},
+            device_id_type=MESH,
+        )
+
     pack(0)
-    pl.semaphore_wait(barrier, n)
+    pl.semaphore_wait(barrier, n + 1 if proxy else n)
     for g in range(2):
         if g == 1:
             pack(1)
 
         @pl.loop(1, n)
         def _(off):
-            exchange(g, off)[0].start()
+            if g == 0 or not proxy:
+                exchange(g, off)[0].start()
+            else:
+                d = lax.rem(me + off, n)
+                to_end_run = (d == 0) | (d == n - 1)
+
+                @pl.when(jnp.logical_not(to_end_run))
+                def _():
+                    exchange(1, off)[0].start()
+
+                @pl.when(to_end_run & (jnp.clip(d, 1, n - 2) != me))
+                def _():
+                    to_helper(off, d).start()
+
+    if proxy:
+
+        @pl.when(at_end)
+        def _():
+            to_helper(0, me).start()
+            ints_piece(0).start()
+
+        @pl.when(is_helper)
+        def _():
+            for j in range(most):
+                for h in range(2):
+                    pool_end[h, me * most + j] = amps[1, send_tab[1, end * (most + 1) + j], h]
 
     for g in range(2):
         for j in range(most):
@@ -175,8 +301,7 @@
     def own(t):
         return pl.ds(pl.multiple_of(t * chunk, chunk), chunk)
 
-    for g in range(2):
-
+    def gather_direct(g):
         @pl.loop(1, n)
         def _(off):
             arrive, pass_on = exchange(g, off)
@@ -187,40 +312,115 @@
         def _(off):
             exchange(g, off)[1].wait_recv()
 
+    def pick_rows(row, pool, hi_ref, lo_ref):
         @pl.loop(0, slots)
         def _(k):
-            where = pick_tab[g, k]
-            tile = jnp.concatenate([pools[g][0, where], pools[g][1, where]], axis=0)
+            where = pick_tab[row, k]
+            tile = jnp.concatenate([pool[0, where], pool[1, where]], axis=0)
             high, low = split(tile)
             at = pl.ds(pl.multiple_of(k * TILE, TILE), TILE)
-            amp_hi[g, at, :] = high
-            amp_lo[g, at, :] = low
+            hi_ref[at, :] = high
+            lo_ref[at, :] = low
+
+    def product(hi_ref, lo_ref, a_hi, a_lo, at):
+        dot = functools.partial(jnp.dot, preferred_element_type=jnp.float32)
+        return (
+            dot(hi_ref[at, :], a_lo[...])
+            + dot(lo_ref[at, :], a_hi[...])
+            + dot(hi_ref[at, :], a_hi[...])
+        )
+
+    for g in range(2):
+        if g == 0 or not proxy:
+            gather_direct(g)
+        else:
+
+            @pl.when(is_helper)
+            def _():
+                @pl.loop(0, n)
+                def _(home):
+                    @pl.when(home != me)
+                    def _():
+                        to_helper_in = pltpu.make_async_remote_copy(
+                            src_ref=packed.at[1, 0],
+                            dst_ref=pool_end.at[core, pl.ds(home * most, most)],
+                            send_sem=p_send.at[home],
+                            recv_sem=p_recv.at[home],
+                            device_id={"pair": end},
+                            device_id_type=MESH,
+                        )
+                        to_helper_in.wait_recv()
+                        end_pass(home).start()
+
+                to_end().start()
+
+            @pl.when(at_end)
+            def _():
+                to_end().wait_recv()
+                end_share().start()
+                end_share().wait_recv()
+
+            @pl.when(jnp.logical_not(at_end))
+            def _():
+                gather_direct(1)
+
+            @pl.when(is_helper)
+            def _():
+                @pl.loop(0, n)
+                def _(home):
+                    @pl.when(home != me)
+                    def _():
+                        end_pass(home).wait_recv()
+
+                @pl.loop(0, n - 1)
+                def _(i):
+                    ints_piece(i).wait_recv()
+                    ints_across(i).start()
+
+                pick_rows(2, pool_end, end_amp_hi, end_amp_lo)
+
+        pick_rows(g, pools[g], amp_hi.at[g], amp_lo.at[g])
+        if g == 0 and proxy:
+
+            @pl.when(at_end)
+            def _():
+                @pl.loop(1, n - 1)
+                def _(i):
+                    ints_piece(i).start()
 
         @pl.loop(0, BLOCKS)
         def _(i):
             b = jnp.where(me < n // 2, BLOCKS - 1 - i, i)
             at = pl.ds(pl.multiple_of(b * block, block), block)
-            dot = functools.partial(jnp.dot, preferred_element_type=jnp.float32)
-            part[g, at, :] = (
-                dot(ints_hi[g, at, :], amp_lo[g])
-                + dot(ints_lo[g, at, :], amp_hi[g])
-                + dot(ints_hi[g, at, :], amp_hi[g])
+            part[g, at, :] = product(
+                ints_hi.at[g], ints_lo.at[g], amp_hi.at[g], amp_lo.at[g], at
             )
+            if g == 1 and proxy:
+
+                @pl.when(is_helper & (i < n - 1))
+                def _():
+                    ints_across(i).wait_recv()
+                    high, low = split(end_ints[i].T)
+                    end_hi[...] = high
+                    end_lo[...] = low
+                    part[g, at, :] = part[g, at, :] + product(
+                        end_hi, end_lo, end_amp_hi, end_amp_lo, pl.ds(0, chunk)
+                    )
 
             @pl.loop(0, per_block)
             def _(j):
                 t = b * per_block + jnp.where(me < n // 2, per_block - 1 - j, j)
 
-                @pl.when((me == 0) & (t > 0))
+                @pl.when((me == first_right[g]) & (t > me))
                 def _():
                     send_right(g, t, part.at[g, own(t)]).start()
 
-                @pl.when((me == n - 1) & (t < n - 1))
+                @pl.when((me == first_left[g]) & (t < me))
                 def _():
                     send_left(g, t, part.at[g, own(t)]).start()
 
     def forward_right(g, t):
-        @pl.when((t > me) & (me > 0))
+        @pl.when((t > me) & (me > first_right[g]))
         def _():
             copy = send_right(g, t, from_left.at[g, t])
             copy.wait_recv()
@@ -228,7 +428,7 @@
             copy.start()
 
     def forward_left(g, t):
-        @pl.when((t < me) & (me < n - 1))
+        @pl.when((t < me) & (me < first_left[g]))
         def _():
             copy = send_left(g, t, from_right.at[g, t])
             copy.wait_recv()
@@ -250,50 +450,86 @@
                 forward_right(g, n - 1 - i)
 
     for g in range(2):
-        out[g] = part[g, own(me), :]
-
-        @pl.when(me > 0)
+        @pl.when(me > first_right[g])
         def _():
             send_right(g, me, from_left.at[g, me]).wait_recv()
-            out[g] = out[g] + from_left[g, me]
-
-        @pl.when(me < n - 1)
+            part[g, own(me), :] = part[g, own(me), :] + from_left[g, me]
+
+        @pl.when(me < first_left[g])
         def _():
             send_left(g, me, from_right.at[g, me]).wait_recv()
-            out[g] = out[g] + from_right[g, me]
+            part[g, own(me), :] = part[g, own(me), :] + from_right[g, me]
+
+        out[:, g, :] = part[g, own(me), :]
 
     for g in range(2):
 
         @pl.loop(1, n)
         def _(off):
-            arrive, pass_on = exchange(g, off)
-            arrive.wait_send()
-            pass_on.wait_send()
+            if g == 0 or not proxy:
+                exchange(g, off)[0].wait_send()
+                exchange(g, off)[1].wait_send()
+            else:
+                d = lax.rem(me + off, n)
+
+                @pl.when(((d != 0) & (d != n - 1)) | (jnp.clip(d, 1, n - 2) != me))
+                def _():
+                    exchange(1, off)[0].wait_send()
+
+                @pl.when(jnp.logical_not(at_end))
+                def _():
+                    exchange(1, off)[1].wait_send()
 
         @pl.loop(0, n)
         def _(t):
-            @pl.when(t > me)
+            @pl.when((t > me) & (me >= first_right[g]))
             def _():
                 send_right(g, t, from_left.at[g, t]).wait_send()
 
-            @pl.when(t < me)
+            @pl.when((t < me) & (me <= first_left[g]))
             def _():
                 send_left(g, t, from_right.at[g, t]).wait_send()
 
-
-def local(n, amplitudes, integrals, tile_map, residual):
+    if proxy:
+
+        @pl.when(at_end)
+        def _():
+            to_helper(0, me).wait_send()
+            end_share().wait_send()
+
+            @pl.loop(0, n - 1)
+            def _(i):
+                ints_piece(i).wait_send()
+
+        @pl.when(is_helper)
+        def _():
+            to_end().wait_send()
+
+            @pl.loop(0, n)
+            def _(home):
+                @pl.when(home != me)
+                def _():
+                    end_pass(home).wait_send()
+
+            @pl.loop(0, n - 1)
+            def _(i):
+                ints_across(i).wait_send()
+
+
+def local(n, columns, amplitudes, integrals, tile_map, residual):
     depth, occ = amplitudes.shape[1:]
     rows = integrals.shape[2]
     slots = depth // TILE
     most = (slots + n - 1) // n
     chunk = rows // n
+    proxy = n == BLOCKS and columns == 2 and chunk % 128 == 0
     smem = pl.BlockSpec(memory_space=pltpu.SMEM)
     vmem = pl.BlockSpec(memory_space=pltpu.VMEM)
     send_tab, pick_tab = pl.pallas_call(
         functools.partial(table_kernel, n, most),
         out_shape=(
             jax.ShapeDtypeStruct((2, n * (most + 1)), jnp.int32),
-            jax.ShapeDtypeStruct((2, slots), jnp.int32),
+            jax.ShapeDtypeStruct((3, slots), jnp.int32),
         ),
         in_specs=[smem],
         out_specs=(smem, smem),
@@ -303,8 +539,8 @@
     dma = pltpu.SemaphoreType.DMA
     flops = 2 * 3 * 2 * depth * rows * occ
     summed = pl.pallas_call(
-        functools.partial(ladder_kernel, n, most),
-        out_shape=jax.ShapeDtypeStruct((2, chunk, occ), f32),
+        functools.partial(ladder_kernel, n, most, proxy),
+        out_shape=jax.ShapeDtypeStruct((chunk, 2, occ), f32),
         in_specs=[smem, smem, vmem, pl.BlockSpec(memory_space=pl.ANY)],
         out_specs=vmem,
         scratch_shapes=[
@@ -319,9 +555,17 @@
             pltpu.VMEM((2, rows, occ), f32),
             pltpu.VMEM((2, n, chunk, occ), f32),
             pltpu.VMEM((2, n, chunk, occ), f32),
+            pltpu.VMEM((2, n * most, HALF, occ), f32),
+            pltpu.VMEM((n - 1, depth, chunk) if proxy else (1, 8, 128), f32),
+            pltpu.VMEM((chunk, depth) if proxy else (16, 128), bf16),
+            pltpu.VMEM((chunk, depth) if proxy else (16, 128), bf16),
+            pltpu.VMEM((depth, occ), bf16),
+            pltpu.VMEM((depth, occ), bf16),
             dma((2,)),
         ]
-        + [dma((2, n))] * 8,
+        + [dma((2, n))] * 8
+        + [dma((n,))] * 8
+        + [dma((4,))],
         compiler_params=pltpu.CompilerParams(
             collective_id=0, has_side_effects=True, vmem_limit_bytes=56 * 1024 * 1024
         ),
@@ -334,7 +578,7 @@
         amplitudes.reshape(2, slots, 2, HALF, occ),
         integrals,
     )
-    return residual + 0.5 * jnp.transpose(summed, (1, 0, 2))[None]
+    return residual + 0.5 * summed[None]
 
 
 def solution(mesh):
@@ -345,7 +589,7 @@
         P("rep", "pair", "groups", "amp"),
     )
     return jax.shard_map(
-        functools.partial(local, mesh.shape["pair"]),
+        functools.partial(local, mesh.shape["pair"], mesh.shape["amp"]),
         mesh=mesh,
         in_specs=placed,
         out_specs=P("rep", "pair", "groups", "amp"),

time: 84.6 us -> 86.5 us (1.022)
  Pallas kernels: 81.7 us -> 83.8 us
  local copies, waits for them, and re-layouts: 1.49 us -> 0.01 us
  other arithmetic: 1.23 us -> 2.52 us
    pallas_call x1, Pallas kernels: 79 us -> 80.9 us  [local(): pl.pallas_call(functools.partial(ladder_kernel, n, most, proxy), out_shap...]
    add x1 -> x0, local copies, waits for them, and re-layouts: 1.49 us -> none  [local(): return residual + 0.5 * jnp.transpose(summed, (1, 0, 2))[None]]
    add x1, other arithmetic: 1.23 us -> 2.52 us  [local(): return residual + 0.5 * summed[None]]
where the time goes in v2:
time: 86.5 us; the launch traced here: 86.3 us
  Pallas kernels  83.8 us (97%)
  other arithmetic  2.52 us (3%)
    pallas_call x1, Pallas kernels, local(): pl.pallas_call(functools.partial(ladder_kernel, n, most, proxy), out_shap...  80.9 us
    pallas_call x1, Pallas kernels, local(): pl.pallas_call(functools.partial(table_kernel, n, most), out_shape=(jax.S...  2.89 us
    add x1, other arithmetic, local(): return residual + 0.5 * summed[None]  2.52 us

profile of v2, /device:TPU:0, one launch (start us, length us, event | category | flops | bytes accessed | tf_op | source)
XLA Modules:
  0.0 86.3 jit_solution(7739186413852017818)
XLA Ops:
  0.0 2.9 %shard_map.46 = (s32[2,32]{1,0:T(2,128)}, s32[3,27]{1,0:T(4,128)}) custom-call(s32[2,108]{1,0:T(2,128)} %map_ref.1), custom_call_target="tpu_custom_call" | custom-call | tf_op jit(solution)/shard_map/pallas_call | solution.py:528
  2.9 0.0 copy-start
  2.9 80.9 %shard_map.47 = f32[256,2,384]{2,1,0:T(2,128)} custom-call(s32[2,32]{1,0:T(2,128)} %get-tuple-element.7.send_tab, s32[3,27]{1,0:T(4,128)} %get-tuple-element.8.pick_tab, f32[2,27,2,8,384]{4,3,2,1,0:T(8,128)} %bitcast.3, f32[2,432,1024]{2,1,0:T(8,128)} %ints_hbm.1), custom_call_target="tpu_custom_call" | custom-call | flops 2038431744 | bytes 4866048 | tf_op jit(solution)/shard_map/pallas_call | solution.py:541
  83.8 0.0 copy-done
  83.8 2.5 %bitcast_add_fusion = f32[1,256,2,384]{3,2,1,0:T(2,128)} fusion(f32[1,256,2,384]{3,2,1,0:T(2,128)S(1)} %copy-done, f32[256,2,384]{2,1,0:T(2,128)} %shard_map.47), kind=kLoop, calls=%fused_computation | loop fusion | flops 393216 | bytes 2359296 | tf_op jit(solution)/shard_map/add | solution.py:581
Async XLA Ops:
  2.9 80.9 %copy-start = (f32[1,256,2,384]{3,2,1,0:T(2,128)S(1)}, f32[1,256,2,384]{3,2,1,0:T(2,128)}, u32[]{:S(2)}) copy-start(f32[1,256,2,384]{3,2,1,0:T(2,128)} %param.7) | copy-start | bytes 2359300

commit v3 on v2

--- a/solution.py
+++ b/solution.py
@@ -228,11 +228,12 @@
             device_id_type=MESH,
         )
 
-    pack(0)
+    order = (1, 0) if proxy else (0, 1)
+    pack(order[0])
     pl.semaphore_wait(barrier, n + 1 if proxy else n)
-    for g in range(2):
-        if g == 1:
-            pack(1)
+    for step, g in enumerate(order):
+        if step == 1:
+            pack(g)
 
         @pl.loop(1, n)
         def _(off):
@@ -250,12 +251,15 @@
                 def _():
                     to_helper(off, d).start()
 
+        if proxy:
+
+            @pl.when(at_end)
+            def _():
+                if g == 1:
+                    to_helper(0, me).start()
+                ints_piece(step).start()
+
     if proxy:
-
-        @pl.when(at_end)
-        def _():
-            to_helper(0, me).start()
-            ints_piece(0).start()
 
         @pl.when(is_helper)
         def _():
@@ -330,94 +334,125 @@
             + dot(hi_ref[at, :], a_hi[...])
         )
 
-    for g in range(2):
-        if g == 0 or not proxy:
+    def near_first(i):
+        return jnp.where(me < n // 2, BLOCKS - 1 - i, i)
+
+    def send_first(g, i):
+        @pl.loop(0, per_block)
+        def _(j):
+            t = near_first(i) * per_block + jnp.where(me < n // 2, per_block - 1 - j, j)
+
+            @pl.when((me == first_right[g]) & (t > me))
+            def _():
+                send_right(g, t, part.at[g, own(t)]).start()
+
+            @pl.when((me == first_left[g]) & (t < me))
+            def _():
+                send_left(g, t, part.at[g, own(t)]).start()
+
+    def multiply(g, b):
+        at = pl.ds(pl.multiple_of(b * block, block), block)
+        part[g, at, :] = product(ints_hi.at[g], ints_lo.at[g], amp_hi.at[g], amp_lo.at[g], at)
+
+    def choose(g):
+        pick_rows(g, pools[g], amp_hi.at[g], amp_lo.at[g])
+
+    def multiply_end(i):
+        ints_across(i).wait_recv()
+        at = own(near_first(i))
+        high, low = split(end_ints[i].T)
+        end_hi[...] = high
+        end_lo[...] = low
+        part[1, at, :] = part[1, at, :] + product(
+            end_hi, end_lo, end_amp_hi, end_amp_lo, pl.ds(0, chunk)
+        )
+
+    def take_piece(i):
+        ints_piece(i).wait_recv()
+        ints_across(i).start()
+
+    if proxy:
+
+        @pl.when(at_end)
+        def _():
+            gather_direct(0)
+            choose(0)
+
+            @pl.loop(0, n)
+            def _(i):
+                @pl.when(i == n - 2)
+                def _():
+                    @pl.loop(2, n - 1)
+                    def _(piece):
+                        ints_piece(piece).start()
+
+                multiply(0, near_first(i))
+                send_first(0, i)
+
+            to_end().wait_recv()
+            end_share().start()
+            end_share().wait_recv()
+            choose(1)
+            multiply(1, me)
+
+        @pl.when(is_helper)
+        def _():
+            @pl.loop(0, n)
+            def _(home):
+                @pl.when(home != me)
+                def _():
+                    to_helper_in = pltpu.make_async_remote_copy(
+                        src_ref=packed.at[1, 0],
+                        dst_ref=pool_end.at[core, pl.ds(home * most, most)],
+                        send_sem=p_send.at[home],
+                        recv_sem=p_recv.at[home],
+                        device_id={"pair": end},
+                        device_id_type=MESH,
+                    )
+                    to_helper_in.wait_recv()
+                    end_pass(home).start()
+
+            gather_direct(1)
+
+            @pl.loop(0, n)
+            def _(home):
+                @pl.when(home != me)
+                def _():
+                    end_pass(home).wait_recv()
+
+            choose(1)
+            pick_rows(2, pool_end, end_amp_hi, end_amp_lo)
+            take_piece(0)
+
+            @pl.loop(0, n)
+            def _(i):
+                multiply(1, near_first(i))
+
+            gather_direct(0)
+            to_end().start()
+            choose(0)
+
+            @pl.loop(0, n)
+            def _(i):
+                multiply(0, near_first(i))
+
+            @pl.loop(0, n - 2)
+            def _(i):
+                @pl.when(i > 0)
+                def _():
+                    take_piece(i)
+
+                multiply_end(i)
+                send_first(1, i)
+    else:
+        for g in range(2):
             gather_direct(g)
-        else:
-
-            @pl.when(is_helper)
-            def _():
-                @pl.loop(0, n)
-                def _(home):
-                    @pl.when(home != me)
-                    def _():
-                        to_helper_in = pltpu.make_async_remote_copy(
-                            src_ref=packed.at[1, 0],
-                            dst_ref=pool_end.at[core, pl.ds(home * most, most)],
-                            send_sem=p_send.at[home],
-                            recv_sem=p_recv.at[home],
-                            device_id={"pair": end},
-                            device_id_type=MESH,
-                        )
-                        to_helper_in.wait_recv()
-                        end_pass(home).start()
-
-                to_end().start()
-
-            @pl.when(at_end)
-            def _():
-                to_end().wait_recv()
-                end_share().start()
-                end_share().wait_recv()
-
-            @pl.when(jnp.logical_not(at_end))
-            def _():
-                gather_direct(1)
-
-            @pl.when(is_helper)
-            def _():
-                @pl.loop(0, n)
-                def _(home):
-                    @pl.when(home != me)
-                    def _():
-                        end_pass(home).wait_recv()
-
-                @pl.loop(0, n - 1)
-                def _(i):
-                    ints_piece(i).wait_recv()
-                    ints_across(i).start()
-
-                pick_rows(2, pool_end, end_amp_hi, end_amp_lo)
-
-        pick_rows(g, pools[g], amp_hi.at[g], amp_lo.at[g])
-        if g == 0 and proxy:
-
-            @pl.when(at_end)
-            def _():
-                @pl.loop(1, n - 1)
-                def _(i):
-                    ints_piece(i).start()
-
-        @pl.loop(0, BLOCKS)
-        def _(i):
-            b = jnp.where(me < n // 2, BLOCKS - 1 - i, i)
-            at = pl.ds(pl.multiple_of(b * block, block), block)
-            part[g, at, :] = product(
-                ints_hi.at[g], ints_lo.at[g], amp_hi.at[g], amp_lo.at[g], at
-            )
-            if g == 1 and proxy:
-
-                @pl.when(is_helper & (i < n - 1))
-                def _():
-                    ints_across(i).wait_recv()
-                    high, low = split(end_ints[i].T)
-                    end_hi[...] = high
-                    end_lo[...] = low
-                    part[g, at, :] = part[g, at, :] + product(
-                        end_hi, end_lo, end_amp_hi, end_amp_lo, pl.ds(0, chunk)
-                    )
-
-            @pl.loop(0, per_block)
-            def _(j):
-                t = b * per_block + jnp.where(me < n // 2, per_block - 1 - j, j)
-
-                @pl.when((me == first_right[g]) & (t > me))
-                def _():
-                    send_right(g, t, part.at[g, own(t)]).start()
-
-                @pl.when((me == first_left[g]) & (t < me))
-                def _():
-                    send_left(g, t, part.at[g, own(t)]).start()
+            choose(g)
+
+            @pl.loop(0, BLOCKS)
+            def _(i):
+                multiply(g, near_first(i))
+                send_first(g, i)
 
     def forward_right(g, t):
         @pl.when((t > me) & (me > first_right[g]))
@@ -449,7 +484,15 @@
                 forward_left(g, i)
                 forward_right(g, n - 1 - i)
 
+    if proxy:
+
+        @pl.when(is_helper)
+        def _():
+            take_piece(n - 2)
+            multiply_end(n - 2)
+
     for g in range(2):
+
         @pl.when(me > first_right[g])
         def _():
             send_right(g, me, from_left.at[g, me]).wait_recv()

time: 86.5 us -> 84 us (0.971)
  Pallas kernels: 83.8 us -> 81.2 us
    pallas_call x1, Pallas kernels: 80.9 us -> 78.3 us  [local(): pl.pallas_call(functools.partial(ladder_kernel, n, most, proxy), out_shap...]
where the time goes in v3:
time: 84 us; the launch traced here: 83.8 us
  Pallas kernels  81.2 us (97%)
  other arithmetic  2.52 us (3%)
    pallas_call x1, Pallas kernels, local(): pl.pallas_call(functools.partial(ladder_kernel, n, most, proxy), out_shap...  78.3 us
    pallas_call x1, Pallas kernels, local(): pl.pallas_call(functools.partial(table_kernel, n, most), out_shape=(jax.S...  2.89 us
    add x1, other arithmetic, local(): return residual + 0.5 * summed[None]  2.52 us

profile of v3, /device:TPU:0, one launch (start us, length us, event | category | flops | bytes accessed | tf_op | source)
XLA Modules:
  0.0 83.8 jit_solution(11538729070831139545)
XLA Ops:
  0.0 2.9 %shard_map.46 = (s32[2,32]{1,0:T(2,128)}, s32[3,27]{1,0:T(4,128)}) custom-call(s32[2,108]{1,0:T(2,128)} %map_ref.1), custom_call_target="tpu_custom_call" | custom-call | tf_op jit(solution)/shard_map/pallas_call | solution.py:571
  2.9 0.0 copy-start
  2.9 78.3 %shard_map.47 = f32[256,2,384]{2,1,0:T(2,128)} custom-call(s32[2,32]{1,0:T(2,128)} %get-tuple-element.7.send_tab, s32[3,27]{1,0:T(4,128)} %get-tuple-element.8.pick_tab, f32[2,27,2,8,384]{4,3,2,1,0:T(8,128)} %bitcast.3, f32[2,432,1024]{2,1,0:T(8,128)} %ints_hbm.1), custom_call_target="tpu_custom_call" | custom-call | flops 2038431744 | bytes 4866048 | tf_op jit(solution)/shard_map/pallas_call | solution.py:584
  81.3 0.0 copy-done
  81.3 2.5 %bitcast_add_fusion = f32[1,256,2,384]{3,2,1,0:T(2,128)} fusion(f32[1,256,2,384]{3,2,1,0:T(2,128)S(1)} %copy-done, f32[256,2,384]{2,1,0:T(2,128)} %shard_map.47), kind=kLoop, calls=%fused_computation | loop fusion | flops 393216 | bytes 2359296 | tf_op jit(solution)/shard_map/add | solution.py:624
Async XLA Ops:
  2.9 78.4 %copy-start = (f32[1,256,2,384]{3,2,1,0:T(2,128)S(1)}, f32[1,256,2,384]{3,2,1,0:T(2,128)}, u32[]{:S(2)}) copy-start(f32[1,256,2,384]{3,2,1,0:T(2,128)} %param.7) | copy-start | bytes 2359300

commit v4 on v3

--- a/solution.py
+++ b/solution.py
@@ -60,6 +60,7 @@
     pick_tab,
     amps,
     ints_hbm,
+    residual,
     out,
     ints,
     packed,
@@ -257,7 +258,8 @@
             def _():
                 if g == 1:
                     to_helper(0, me).start()
-                ints_piece(step).start()
+                for i in (range(1, n - 1) if step == 1 else range(1)):
+                    ints_piece(i).start()
 
     if proxy:
 
@@ -380,12 +382,6 @@
 
             @pl.loop(0, n)
             def _(i):
-                @pl.when(i == n - 2)
-                def _():
-                    @pl.loop(2, n - 1)
-                    def _(piece):
-                        ints_piece(piece).start()
-
                 multiply(0, near_first(i))
                 send_first(0, i)
 
@@ -428,6 +424,8 @@
             def _(i):
                 multiply(1, near_first(i))
 
+            multiply_end(0)
+            send_first(1, 0)
             gather_direct(0)
             to_end().start()
             choose(0)
@@ -436,12 +434,9 @@
             def _(i):
                 multiply(0, near_first(i))
 
-            @pl.loop(0, n - 2)
+            @pl.loop(1, n - 2)
             def _(i):
-                @pl.when(i > 0)
-                def _():
-                    take_piece(i)
-
+                take_piece(i)
                 multiply_end(i)
                 send_first(1, i)
     else:
@@ -503,7 +498,7 @@
             send_left(g, me, from_right.at[g, me]).wait_recv()
             part[g, own(me), :] = part[g, own(me), :] + from_right[g, me]
 
-        out[:, g, :] = part[g, own(me), :]
+        out[:, g, :] = residual[:, g, :] + 0.5 * part[g, own(me), :]
 
     for g in range(2):
 
@@ -584,7 +579,7 @@
     summed = pl.pallas_call(
         functools.partial(ladder_kernel, n, most, proxy),
         out_shape=jax.ShapeDtypeStruct((chunk, 2, occ), f32),
-        in_specs=[smem, smem, vmem, pl.BlockSpec(memory_space=pl.ANY)],
+        in_specs=[smem, smem, vmem, pl.BlockSpec(memory_space=pl.ANY), vmem],
         out_specs=vmem,
         scratch_shapes=[
             pltpu.VMEM((2, depth, rows), f32),
@@ -620,8 +615,9 @@
         pick_tab,
         amplitudes.reshape(2, slots, 2, HALF, occ),
         integrals,
+        residual[0],
     )
-    return residual + 0.5 * summed[None]
+    return summed[None]
 
 
 def solution(mesh):

time: 84 us -> 81 us (0.964)
  Pallas kernels: 81.2 us -> 78.5 us
  other arithmetic: 2.52 us -> 0 us
  local copies, waits for them, and re-layouts: 0.01 us -> 2.28 us
    pallas_call x1, Pallas kernels: 78.3 us -> 75.6 us  [local(): pl.pallas_call(functools.partial(ladder_kernel, n, most, proxy), out_shap...]
    add x1 -> x0, other arithmetic: 2.52 us -> none  [local(): return residual + 0.5 * summed[None]]
    unnamed x2 -> x1, local copies, waits for them, and re-layouts: 0.01 us -> 2.28 us
where the time goes in v4:
time: 81 us; the launch traced here: 80.8 us
  Pallas kernels  78.5 us (97%)
  local copies, waits for them, and re-layouts  2.28 us (3%)
    pallas_call x1, Pallas kernels, local(): pl.pallas_call(functools.partial(ladder_kernel, n, most, proxy), out_shap...  75.6 us
    pallas_call x1, Pallas kernels, local(): pl.pallas_call(functools.partial(table_kernel, n, most), out_shape=(jax.S...  2.89 us
    unnamed x1, local copies, waits for them, and re-layouts  2.28 us

profile of v4, /device:TPU:0, one launch (start us, length us, event | category | flops | bytes accessed | tf_op | source)
XLA Modules:
  0.0 80.8 jit_solution(18015445695794865778)
XLA Ops:
  0.0 2.9 %shard_map.46 = (s32[2,32]{1,0:T(2,128)}, s32[3,27]{1,0:T(4,128)}) custom-call(s32[2,108]{1,0:T(2,128)} %map_ref.1), custom_call_target="tpu_custom_call" | custom-call | tf_op jit(solution)/shard_map/pallas_call | solution.py:566
  2.9 75.6 %shard_map.47 = f32[256,2,384]{2,1,0:T(2,128)} custom-call(s32[2,32]{1,0:T(2,128)} %get-tuple-element.7.send_tab, s32[3,27]{1,0:T(4,128)} %get-tuple-element.8.pick_tab, f32[2,27,2,8,384]{4,3,2,1,0:T(8,128)} %bitcast.4, f32[2,432,1024]{2,1,0:T(8,128)} %ints_hbm.1, f32[256,2,384]{2,1,0:T(2,128)} %bitcast.5), custom_call_target="tpu_custom_call" | custom-call | flops 2038431744 | bytes 4866048 | tf_op jit(solution)/shard_map/pallas_call | solution.py:579
  78.5 2.3 %copy.6 = f32[1,256,2,384]{3,2,1,0:T(2,128)} copy(f32[1,256,2,384]{3,2,1,0:T(2,128)} %bitcast.3) | data formatting | bytes 1572864

commit v5 on v4

--- a/solution.py
+++ b/solution.py
@@ -284,28 +284,35 @@
             ints_hi[g, columns, :] = high
             ints_lo[g, columns, :] = low
 
-    def send_right(g, t, src):
+    def send_right(g, t, u, src):
         return pltpu.make_async_remote_copy(
             src_ref=src,
-            dst_ref=from_left.at[g, t],
-            send_sem=r_send.at[g, t],
-            recv_sem=r_recv.at[g, t],
+            dst_ref=from_left.at[g, t, piece(u)],
+            send_sem=r_send.at[g, t * 2 + u],
+            recv_sem=r_recv.at[g, t * 2 + u],
             device_id={"pair": lax.rem(me + 1, n)},
             device_id_type=MESH,
         )
 
-    def send_left(g, t, src):
+    def send_left(g, t, u, src):
         return pltpu.make_async_remote_copy(
             src_ref=src,
-            dst_ref=from_right.at[g, t],
-            send_sem=l_send.at[g, t],
-            recv_sem=l_recv.at[g, t],
+            dst_ref=from_right.at[g, t, piece(u)],
+            send_sem=l_send.at[g, t * 2 + u],
+            recv_sem=l_recv.at[g, t * 2 + u],
             device_id={"pair": lax.rem(me - 1 + n, n)},
             device_id_type=MESH,
         )
 
-    def own(t):
-        return pl.ds(pl.multiple_of(t * chunk, chunk), chunk)
+    half = chunk // 2
+
+    def own(t, u=None):
+        if u is None:
+            return pl.ds(pl.multiple_of(t * chunk, chunk), chunk)
+        return pl.ds(pl.multiple_of(t * chunk + u * half, half), half)
+
+    def piece(u):
+        return pl.ds(u * half, half)
 
     def gather_direct(g):
         @pl.loop(1, n)
@@ -346,11 +353,13 @@
 
             @pl.when((me == first_right[g]) & (t > me))
             def _():
-                send_right(g, t, part.at[g, own(t)]).start()
+                for u in range(2):
+                    send_right(g, t, u, part.at[g, own(t, u)]).start()
 
             @pl.when((me == first_left[g]) & (t < me))
             def _():
-                send_left(g, t, part.at[g, own(t)]).start()
+                for u in range(2):
+                    send_left(g, t, u, part.at[g, own(t, u)]).start()
 
     def multiply(g, b):
         at = pl.ds(pl.multiple_of(b * block, block), block)
@@ -434,7 +443,7 @@
             def _(i):
                 multiply(0, near_first(i))
 
-            @pl.loop(1, n - 2)
+            @pl.loop(1, n - 1)
             def _(i):
                 take_piece(i)
                 multiply_end(i)
@@ -452,18 +461,20 @@
     def forward_right(g, t):
         @pl.when((t > me) & (me > first_right[g]))
         def _():
-            copy = send_right(g, t, from_left.at[g, t])
-            copy.wait_recv()
-            from_left[g, t] = from_left[g, t] + part[g, own(t), :]
-            copy.start()
+            for u in range(2):
+                copy = send_right(g, t, u, from_left.at[g, t, piece(u)])
+                copy.wait_recv()
+                from_left[g, t, piece(u)] = from_left[g, t, piece(u)] + part[g, own(t, u), :]
+                copy.start()
 
     def forward_left(g, t):
         @pl.when((t < me) & (me < first_left[g]))
         def _():
-            copy = send_left(g, t, from_right.at[g, t])
-            copy.wait_recv()
-            from_right[g, t] = from_right[g, t] + part[g, own(t), :]
-            copy.start()
+            for u in range(2):
+                copy = send_left(g, t, u, from_right.at[g, t, piece(u)])
+                copy.wait_recv()
+                from_right[g, t, piece(u)] = from_right[g, t, piece(u)] + part[g, own(t, u), :]
+                copy.start()
 
     for g in range(2):
 
@@ -479,23 +490,18 @@
                 forward_left(g, i)
                 forward_right(g, n - 1 - i)
 
-    if proxy:
-
-        @pl.when(is_helper)
-        def _():
-            take_piece(n - 2)
-            multiply_end(n - 2)
-
     for g in range(2):
 
         @pl.when(me > first_right[g])
         def _():
-            send_right(g, me, from_left.at[g, me]).wait_recv()
+            for u in range(2):
+                send_right(g, me, u, from_left.at[g, me, piece(u)]).wait_recv()
             part[g, own(me), :] = part[g, own(me), :] + from_left[g, me]
 
         @pl.when(me < first_left[g])
         def _():
-            send_left(g, me, from_right.at[g, me]).wait_recv()
+            for u in range(2):
+                send_left(g, me, u, from_right.at[g, me, piece(u)]).wait_recv()
             part[g, own(me), :] = part[g, own(me), :] + from_right[g, me]
 
         out[:, g, :] = residual[:, g, :] + 0.5 * part[g, own(me), :]
@@ -522,11 +528,13 @@
         def _(t):
             @pl.when((t > me) & (me >= first_right[g]))
             def _():
-                send_right(g, t, from_left.at[g, t]).wait_send()
+                for u in range(2):
+                    send_right(g, t, u, from_left.at[g, t, piece(u)]).wait_send()
 
             @pl.when((t < me) & (me <= first_left[g]))
             def _():
-                send_left(g, t, from_right.at[g, t]).wait_send()
+                for u in range(2):
+                    send_left(g, t, u, from_right.at[g, t, piece(u)]).wait_send()
 
     if proxy:
 
@@ -601,7 +609,8 @@
             pltpu.VMEM((depth, occ), bf16),
             dma((2,)),
         ]
-        + [dma((2, n))] * 8
+        + [dma((2, n))] * 4
+        + [dma((2, 2 * n))] * 4
         + [dma((n,))] * 8
         + [dma((4,))],
         compiler_params=pltpu.CompilerParams(

time: 81 us -> 78.3 us (0.967)
  Pallas kernels: 78.5 us -> 75.8 us
    pallas_call x1, Pallas kernels: 75.6 us -> 73 us  [local(): pl.pallas_call(functools.partial(ladder_kernel, n, most, proxy), out_shap...]
where the time goes in v5:
time: 78.3 us; the launch traced here: 78.1 us
  Pallas kernels  75.8 us (97%)
  local copies, waits for them, and re-layouts  2.28 us (3%)
    pallas_call x1, Pallas kernels, local(): pl.pallas_call(functools.partial(ladder_kernel, n, most, proxy), out_shap...  73 us
    pallas_call x1, Pallas kernels, local(): pl.pallas_call(functools.partial(table_kernel, n, most), out_shape=(jax.S...  2.89 us
    unnamed x1, local copies, waits for them, and re-layouts  2.28 us

profile of v5, /device:TPU:0, one launch (start us, length us, event | category | flops | bytes accessed | tf_op | source)
XLA Modules:
  0.0 78.1 jit_solution(7700724228138444554)
XLA Ops:
  0.0 2.9 %shard_map.46 = (s32[2,32]{1,0:T(2,128)}, s32[3,27]{1,0:T(4,128)}) custom-call(s32[2,108]{1,0:T(2,128)} %map_ref.1), custom_call_target="tpu_custom_call" | custom-call | tf_op jit(solution)/shard_map/pallas_call | solution.py:574
  2.9 73.0 %shard_map.47 = f32[256,2,384]{2,1,0:T(2,128)} custom-call(s32[2,32]{1,0:T(2,128)} %get-tuple-element.7.send_tab, s32[3,27]{1,0:T(4,128)} %get-tuple-element.8.pick_tab, f32[2,27,2,8,384]{4,3,2,1,0:T(8,128)} %bitcast.4, f32[2,432,1024]{2,1,0:T(8,128)} %ints_hbm.1, f32[256,2,384]{2,1,0:T(2,128)} %bitcast.5), custom_call_target="tpu_custom_call" | custom-call | flops 2038431744 | bytes 4866048 | tf_op jit(solution)/shard_map/pallas_call | solution.py:587
  75.9 2.3 %copy.6 = f32[1,256,2,384]{3,2,1,0:T(2,128)} copy(f32[1,256,2,384]{3,2,1,0:T(2,128)} %bitcast.3) | data formatting | bytes 1572864

commit v6 on v5

--- a/solution.py
+++ b/solution.py
@@ -425,16 +425,17 @@
                 def _():
                     end_pass(home).wait_recv()
 
+            take_piece(0)
             choose(1)
             pick_rows(2, pool_end, end_amp_hi, end_amp_lo)
-            take_piece(0)
-
-            @pl.loop(0, n)
+            multiply(1, near_first(0))
+            multiply_end(0)
+            send_first(1, 0)
+
+            @pl.loop(1, n)
             def _(i):
                 multiply(1, near_first(i))
 
-            multiply_end(0)
-            send_first(1, 0)
             gather_direct(0)
             to_end().start()
             choose(0)

time: 78.3 us -> 79.9 us (1.020)
  Pallas kernels: 75.8 us -> 77.4 us
    pallas_call x1, Pallas kernels: 73 us -> 74.5 us  [local(): pl.pallas_call(functools.partial(ladder_kernel, n, most, proxy), out_shap...]
where the time goes in v6:
time: 79.9 us; the launch traced here: 79.7 us
  Pallas kernels  77.4 us (97%)
  local copies, waits for them, and re-layouts  2.28 us (3%)
    pallas_call x1, Pallas kernels, local(): pl.pallas_call(functools.partial(ladder_kernel, n, most, proxy), out_shap...  74.5 us
    pallas_call x1, Pallas kernels, local(): pl.pallas_call(functools.partial(table_kernel, n, most), out_shape=(jax.S...  2.89 us
    unnamed x1, local copies, waits for them, and re-layouts  2.28 us

profile of v6, /device:TPU:0, one launch (start us, length us, event | category | flops | bytes accessed | tf_op | source)
XLA Modules:
  0.0 79.7 jit_solution(15803098429973066359)
XLA Ops:
  0.0 2.9 %shard_map.46 = (s32[2,32]{1,0:T(2,128)}, s32[3,27]{1,0:T(4,128)}) custom-call(s32[2,108]{1,0:T(2,128)} %map_ref.1), custom_call_target="tpu_custom_call" | custom-call | tf_op jit(solution)/shard_map/pallas_call | solution.py:575
  2.9 74.5 %shard_map.47 = f32[256,2,384]{2,1,0:T(2,128)} custom-call(s32[2,32]{1,0:T(2,128)} %get-tuple-element.7.send_tab, s32[3,27]{1,0:T(4,128)} %get-tuple-element.8.pick_tab, f32[2,27,2,8,384]{4,3,2,1,0:T(8,128)} %bitcast.4, f32[2,432,1024]{2,1,0:T(8,128)} %ints_hbm.1, f32[256,2,384]{2,1,0:T(2,128)} %bitcast.5), custom_call_target="tpu_custom_call" | custom-call | flops 2038431744 | bytes 4866048 | tf_op jit(solution)/shard_map/pallas_call | solution.py:588
  77.4 2.3 %copy.6 = f32[1,256,2,384]{3,2,1,0:T(2,128)} copy(f32[1,256,2,384]{3,2,1,0:T(2,128)} %bitcast.3) | data formatting | bytes 1572864
